TPU v7x, 32 devices: a whole 2x2x4 slice. The times are simulated.
32 devices in a mesh: gx: 16 (over z, y, core), gy: 2 (over x).
Axes of the slice: x: 2, y: 2, z: 4, core: 2. Of those that a mesh axis runs over, the one named last changes fastest.
Arguments:
- velocity_x: bfloat16 [256, 128, 128], P('gx', 'gy'), may hold values from -6 to 6
- velocity_y: bfloat16 [256, 128, 128], P('gx', 'gy'), may hold values from -6 to 6
- velocity_z: bfloat16 [256, 128, 128], P('gx', 'gy'), may hold values from -6 to 6
- potential_temp: bfloat16 [256, 128, 128], P('gx', 'gy'), may hold values from -6 to 6
- total_water: bfloat16 [256, 128, 128], P('gx', 'gy'), may hold values from -6 to 6
Outputs:
- wind_x_next: bfloat16 [256, 128, 128], P('gx', 'gy')
- wind_y_next: bfloat16 [256, 128, 128], P('gx', 'gy')
- wind_z_next: bfloat16 [256, 128, 128], P('gx', 'gy')
- temp_next: bfloat16 [256, 128, 128], P('gx', 'gy')
- water_next: bfloat16 [256, 128, 128], P('gx', 'gy')
- pressure: float32 [256, 128, 128], P('gx', 'gy')
All inputs are finite; a program needn't handle non-finite values.
Results may differ from a plain program's by a relative error of at most 0.001.
Values may be sent and summed in bfloat16 or wider, within the bound.
A program may use at most 64 MiB of HBM per device.

v0:
```python
import math

import jax
import jax.numpy as jnp
from jax import lax
from jax.sharding import PartitionSpec as P

time_step = 0.25
diffusion = 0.1
central_coef = (-1.0, 9.0, -45.0, 0.0, 45.0, -9.0, 1.0)
damping_coef = (1.0, -6.0, 15.0, -20.0, 15.0, -6.0, 1.0)
highest = lax.Precision.HIGHEST


def with_halo(cells, sides, width):
    for axis, dim in sides:
        count = lax.axis_size(axis)
        head = lax.slice_in_dim(cells, 0, width, axis=dim)
        tail = lax.slice_in_dim(cells, cells.shape[dim] - width, cells.shape[dim], axis=dim)
        cells = jnp.concatenate(
            [
                lax.ppermute(tail, axis, [(i, (i + 1) % count) for i in range(count)]),
                cells,
                lax.ppermute(head, axis, [((i + 1) % count, i) for i in range(count)]),
            ],
            axis=dim,
        )
    return cells


def tendency(padded_field, speed_x, speed_y, speed_z):
    extent_x, extent_y, levels = speed_x.shape
    extended = jnp.pad(padded_field, ((0, 0), (0, 0), (3, 3)))

    def neighbour(shift_x, shift_y, shift_z):
        return extended[
            3 + shift_x : 3 + shift_x + extent_x,
            3 + shift_y : 3 + shift_y + extent_y,
            3 + shift_z : 3 + shift_z + levels,
        ]

    centre = neighbour(0, 0, 0)
    laplace = -6.0 * centre
    advect = jnp.zeros_like(centre)
    for direction, speed in enumerate((speed_x, speed_y, speed_z)):
        central = jnp.zeros_like(centre)
        damped = jnp.zeros_like(centre)
        for offset in range(-3, 4):
            shifts = [0, 0, 0]
            shifts[direction] = offset
            sample = neighbour(shifts[0], shifts[1], shifts[2])
            central = central + central_coef[offset + 3] * sample
            damped = damped + damping_coef[offset + 3] * sample
            if offset == -1 or offset == 1:
                laplace = laplace + sample
        advect = advect + speed * central / 60.0 - jnp.abs(speed) * damped / 60.0
    return diffusion * laplace - advect


def divergence(extended_x, extended_y, vertical):
    grad_x = (extended_x[2:, 1:-1] - extended_x[:-2, 1:-1]) * 0.5
    grad_y = (extended_y[1:-1, 2:] - extended_y[1:-1, :-2]) * 0.5
    padded_z = jnp.pad(vertical, ((0, 0), (0, 0), (1, 1)))
    grad_z = (padded_z[:, :, 2:] - padded_z[:, :, :-2]) * 0.5
    return (grad_x + grad_y + grad_z) / time_step


def cosine_table(length):
    grid_index = jnp.arange(length, dtype=jnp.int32)[:, None]
    mode_index = jnp.arange(length, dtype=jnp.int32)[None, :]
    angle = (
        math.pi
        / (2.0 * length)
        * (mode_index * (2 * grid_index + 1) % (4 * length)).astype(jnp.float32)
    )
    scaling = jnp.where(mode_index == 0, math.sqrt(1.0 / length), math.sqrt(2.0 / length))
    return jnp.cos(angle) * scaling


def fourier_table(length):
    grid_index = jnp.arange(length, dtype=jnp.int32)[:, None]
    mode_index = jnp.arange(length, dtype=jnp.int32)[None, :]
    halfway = length // 2
    frequency = jnp.where(mode_index <= halfway, mode_index, mode_index - halfway)
    angle = 2.0 * math.pi / length * (grid_index * frequency % length).astype(jnp.float32)
    scaling = jnp.where(
        (mode_index == 0) | (mode_index == halfway),
        math.sqrt(1.0 / length),
        math.sqrt(2.0 / length),
    )
    return jnp.where(mode_index <= halfway, jnp.cos(angle), jnp.sin(angle)) * scaling


def cosine_eigen(mode_index, length):
    return 2.0 * jnp.cos(math.pi / length * mode_index.astype(jnp.float32)) - 2.0


def fourier_eigen(mode_index, length):
    halfway = length // 2
    frequency = jnp.where(mode_index <= halfway, mode_index, mode_index - halfway)
    return 2.0 * jnp.cos(2.0 * math.pi / length * frequency.astype(jnp.float32)) - 2.0


def inverse_factor(eigen, constant):
    return jnp.where(constant, 0.0, 1.0 / jnp.where(constant, 1.0, eigen))


def body(velocity_x, velocity_y, velocity_z, potential_temp, total_water):
    stacked = jnp.stack([velocity_x, velocity_y, velocity_z, potential_temp, total_water])
    padded = with_halo(stacked, (("gx", 1), ("gy", 2)), 4)
    winds = padded[0:3, 3:-3, 3:-3].astype(jnp.float32)
    heating = padded[3, 3:-3, 3:-3].astype(jnp.float32)
    starred = []
    for position in range(3):
        change = tendency(padded[position].astype(jnp.float32), winds[0], winds[1], winds[2])
        if position == 2:
            change = change + heating
        starred.append(winds[position] + time_step * change)
    scalars = []
    for position in range(3, 5):
        change = tendency(
            padded[position, 1:-1, 1:-1].astype(jnp.float32),
            winds[0, 1:-1, 1:-1],
            winds[1, 1:-1, 1:-1],
            winds[2, 1:-1, 1:-1],
        )
        scalars.append(padded[position, 4:-4, 4:-4].astype(jnp.float32) + time_step * change)
    source = divergence(starred[0], starred[1], starred[2][1:-1, 1:-1])
    cells_x, cells_y, levels = source.shape
    count_x = lax.axis_size("gx")
    count_y = lax.axis_size("gy")
    total_x = cells_x * count_x
    total_y = cells_y * count_y
    table_z = cosine_table(levels)
    table_x = fourier_table(total_x)
    table_y = fourier_table(total_y)
    spectral_z = jnp.einsum("xyz,zk->kxy", source, table_z, precision=highest)
    level_part = levels // count_y
    mode_part = total_y // count_x
    lines_y = lax.all_to_all(spectral_z, "gy", split_axis=0, concat_axis=2, tiled=True)
    table_xg = table_x.reshape(count_x, cells_x, total_x)
    table_yg = table_y.reshape(total_y, count_x, mode_part)
    spec_y = jnp.einsum("kxy,ygm->kgmx", lines_y, table_yg, precision=highest)
    packed = spec_y.reshape(level_part, count_x, mode_part * cells_x)
    lines_x = lax.all_to_all(packed, "gx", split_axis=1, concat_axis=0, tiled=True)
    lines_x = lines_x.reshape(count_x, level_part, mode_part, cells_x)
    spec_x = jnp.einsum("gkmx,gxn->kmn", lines_x, table_xg, precision=highest)
    mode_z = lax.axis_index("gy") * level_part + jnp.arange(level_part, dtype=jnp.int32)
    mode_y = lax.axis_index("gx") * mode_part + jnp.arange(mode_part, dtype=jnp.int32)
    mode_x = jnp.arange(total_x, dtype=jnp.int32)
    eigen = (
        cosine_eigen(mode_z, levels)[:, None, None]
        + fourier_eigen(mode_y, total_y)[None, :, None]
        + fourier_eigen(mode_x, total_x)[None, None, :]
    )
    constant = (
        (mode_z == 0)[:, None, None] & (mode_y == 0)[None, :, None] & (mode_x == 0)[None, None, :]
    )
    solved = spec_x * inverse_factor(eigen, constant)
    back_x = jnp.einsum("kmn,gxn->kgmx", solved, table_xg, precision=highest)
    back_x = back_x.reshape(level_part, count_x, mode_part * cells_x)
    returned_x = lax.all_to_all(back_x, "gx", split_axis=1, concat_axis=0, tiled=True)
    returned_x = returned_x.reshape(count_x, level_part, mode_part, cells_x)
    back_y = jnp.einsum("gkmx,ygm->kxy", returned_x, table_yg, precision=highest)
    columns = lax.all_to_all(back_y, "gy", split_axis=2, concat_axis=0, tiled=True)
    pressure = jnp.einsum("kxy,zk->xyz", columns, table_z, precision=highest)
    return (
        starred[0][1:-1, 1:-1].astype(jnp.bfloat16),
        starred[1][1:-1, 1:-1].astype(jnp.bfloat16),
        starred[2][1:-1, 1:-1].astype(jnp.bfloat16),
        scalars[0].astype(jnp.bfloat16),
        scalars[1].astype(jnp.bfloat16),
        pressure,
    )


def solution(mesh):
    placed = (
        P("gx", "gy", None),
        P("gx", "gy", None),
        P("gx", "gy", None),
        P("gx", "gy", None),
        P("gx", "gy", None),
    )
    return jax.shard_map(
        body,
        mesh=mesh,
        in_specs=placed,
        out_specs=(
            P("gx", "gy", None),
            P("gx", "gy", None),
            P("gx", "gy", None),
            P("gx", "gy", None),
            P("gx", "gy", None),
            P("gx", "gy", None),
        ),
        check_vma=False,
    )
```

profile of v0, /device:TPU:0, one launch (start us, length us, event | category | flops | bytes accessed | tf_op | source)
XLA Modules:
  0.0 143.7 jit_solution(5852217624555587488)
XLA Ops:
  5.2 5.1 %collective-permute-start.1 = (bf16[5,4,64,128]{3,2,1,0:T(8,128)(2,1)S(1)}, bf16[5,4,64,128]{3,2,1,0:T(8,128)(2,1)S(1)}, u32[]{:S(2)}, u32[]{:S(2)}) collective-permute-start(bf16[5,4,64,128]{3,2,1,0:T(8,128)(2,1)S(1)} %get-tuple-element.18), channel_id=1, source_target_pairs={{2,0},{4,2},{6,4},{8,6},{10,8},{12,10},{14,12},{16,14},{18,16},{20... | collective-permute-start | bytes 983048 | tf_op jit(solution)/shard_map/ppermute | solution.py:24
  10.4 4.7 %collective-permute-done = bf16[5,4,64,128]{3,2,1,0:T(8,128)(2,1)S(1)} collective-permute-done((bf16[5,4,64,128]{3,2,1,0:T(8,128)(2,1)S(1)}, bf16[5,4,64,128]{3,2,1,0:T(8,128)(2,1)S(1)}, u32[]{:S(2)}, u32[]{:S(2)}) %collective-permute-start) | collective-permute-done | bytes 327712 | tf_op jit(solution)/shard_map/ppermute | solution.py:22
  17.3 2.8 %collective-permute-done.2 = bf16[5,24,4,128]{3,2,1,0:T(4,128)(2,1)S(1)} collective-permute-done((bf16[5,24,4,128]{3,2,1,0:T(4,128)(2,1)S(1)}, bf16[5,24,4,128]{3,2,1,0:T(4,128)(2,1)S(1)}, u32[]{:S(2)}, u32[]{:S(2)}) %collective-permute-start.2) | collective-permute-done | bytes 122912 | tf_op jit(solution)/shard_map/ppermute | solution.py:22
  20.2 3.2 %collective-permute-done.3 = bf16[5,24,4,128]{3,2,1,0:T(4,128)(2,1)S(1)} collective-permute-done((bf16[5,24,4,128]{3,2,1,0:T(4,128)(2,1)S(1)}, bf16[5,24,4,128]{3,2,1,0:T(4,128)(2,1)S(1)}, u32[]{:S(2)}, u32[]{:S(2)}) %collective-permute-start.3) | collective-permute-done | bytes 122912 | tf_op jit(solution)/shard_map/ppermute | solution.py:24
  23.4 2.3 %pad_maximum_fusion = bf16[5,24,72,128]{3,2,1,0:T(8,128)(2,1)S(1)} fusion(bf16[5,24,4,128]{3,2,1,0:T(4,128)(2,1)S(1)} %collective-permute-done.3, bf16[5,4,64,128]{3,2,1,0:T(8,128)(2,1)S(1)} %collective-permute-done.1, bf16[5,16,64,128]{3,2,1,0:T(8,128)(2,1)S(1)} %bitcast_dynamic-update-slice_fusion, bf16[5,4,64,128]{3,2,1,0:T(8,128)(2,1)S(1)} %collective-permute-done, ...), kind=kLoop, calls=%fused_computation.30 | loop fusion | flops 11059200 | bytes 4423680 | tf_op jit(solution)/shard_map/concatenate | solution.py:20
  27.1 2.4 %multiply_subtract_fusion = (f32[18,66,128]{2,1,0:T(8,128)S(1)}, f32[18,66,128]{2,1,0:T(8,128)S(1)}) fusion(f32[24,72,128]{2,1,0:T(8,128)S(1)} %get-tuple-element.12, f32[3,18,66,128]{3,2,1,0:T(8,128)S(1)} %slice_convert_fusion), kind=kLoop, calls=%fused_computation.46 | loop fusion | flops 10492416 | bytes 12718080 | tf_op jit(solution)/shard_map/sub | solution.py:56
  31.0 3.0 %multiply_add_fusion = f32[18,66,128]{2,1,0:T(8,128)S(1)} fusion(f32[24,72,128]{2,1,0:T(8,128)S(1)} %get-tuple-element.13, f32[3,18,66,128]{3,2,1,0:T(8,128)S(1)} %slice_convert_fusion), kind=kLoop, calls=%fused_computation.48 | loop fusion | flops 14598144 | bytes 12109824 | tf_op jit(solution)/shard_map/add | solution.py:118
  34.0 3.1 %multiply_add_fusion.1 = f32[18,66,128]{2,1,0:T(8,128)S(1)} fusion(f32[24,72,128]{2,1,0:T(8,128)S(1)} %get-tuple-element.14, f32[3,18,66,128]{3,2,1,0:T(8,128)S(1)} %slice_convert_fusion), kind=kLoop, calls=%fused_computation.49 | loop fusion | flops 14598144 | bytes 12109824 | tf_op jit(solution)/shard_map/add | solution.py:118
  43.1 3.7 %all-to-all-start = ((f32[2,1,65536]{2,1,0:T(1,128)}), f32[2,1,65536]{2,1,0:T(1,128)S(1)}, u32[]{:S(2)}, u32[]{:S(2)}) async-start(f32[2,1,65536]{2,1,0:T(1,128)} %reshape.367), calls=%async_computation | async-start | bytes 1048576 | tf_op jit(solution)/shard_map/all_to_all | solution.py:140
  47.2 8.7 %all-to-all-done = f32[2,1,65536]{2,1,0:T(1,128)S(1)} async-done(((f32[2,1,65536]{2,1,0:T(1,128)}), f32[2,1,65536]{2,1,0:T(1,128)S(1)}, u32[]{:S(2)}, u32[]{:S(2)}) %all-to-all-start) | async-done | bytes 524320 | tf_op jit(solution)/shard_map/all_to_all | solution.py:140
  56.4 3.0 %reduce = f32[2,65536]{1,0:T(2,128)} reduce(f32[2,1,65536]{2,1,0:T(1,128)S(1)} %all-to-all-done, f32[]{:T(128)} %broadcast.801), dimensions={1}, to_apply=%all_to_all.48.reduce_sub_computation | reduce | bytes 1048580 | tf_op jit(solution)/shard_map/all_to_all | solution.py:140
  67.7 4.1 %all-to-all-start.1 = ((f32[64,16,128]{2,0,1:T(8,128)}), f32[64,16,128]{2,0,1:T(8,128)S(1)}, u32[]{:S(2)}, u32[]{:S(2)}) async-start(f32[64,16,128]{2,0,1:T(8,128)} %copy.34), calls=%async_computation.1 | async-start | bytes 1048576 | tf_op jit(solution)/shard_map/all_to_all | solution.py:145
  72.0 14.2 %all-to-all-done.1 = f32[64,16,128]{2,0,1:T(8,128)S(1)} async-done(((f32[64,16,128]{2,0,1:T(8,128)}), f32[64,16,128]{2,0,1:T(8,128)S(1)}, u32[]{:S(2)}, u32[]{:S(2)}) %all-to-all-start.1) | async-done | bytes 524320 | tf_op jit(solution)/shard_map/all_to_all | solution.py:145
  87.6 4.1 %fusion.1 = f32[64,8,256,1]{2,0,1,3:T(8,128)S(1)} fusion(f32[16,64,8,16]{1,3,2,0:T(8,128)} %bitcast.153, f32[256]{0:T(256)S(1)} %get-tuple-element.23, f32[64,8]{0,1:T(8,128)S(1)} %broadcast_add_fusion, pred[256]{0:T(512)(128)(4,1)S(1)} %get-tuple-element.24, pred[64,8]{0,1:T(8,128)(4,1)S(1)} %broadcast_and_fusion, f32[256]{0:T(256)S(1)} %get-tuple-element.22, ...), kind=kOutput, calls=%fused_computation.37 | convolution fusion | flops 404488192 | bytes 1055744 | tf_op jit(solution)/shard_map/gkmx,gxn->kmn/dot_general | solution.py:147
  91.7 2.1 %fusion.25 = f32[16,16,64,8]{2,1,3,0:T(8,128)S(1)} fusion(f32[64,8,256,1]{2,0,1,3:T(8,128)S(1)} %fusion.1, f32[256]{0:T(256)S(1)} %get-tuple-element.22, s32[256]{0:T(256)S(1)} %add_select_fusion.4, s32[16,16]{1,0:T(8,128)S(1)} %multiply_add_fusion.2, pred[256]{0:T(512)(128)(4,1)S(1)} %get-tuple-element.25), kind=kOutput, calls=%fused_computation.97 | convolution fusion | flops 403701760 | bytes 1051904 | tf_op jit(solution)/shard_map/kmn,gxn->kgmx/dot_general | solution.py:160
  94.9 4.1 %all-to-all-start.2 = ((f32[64,16,128]{2,0,1:T(8,128)}), f32[64,16,128]{2,0,1:T(8,128)S(1)}, u32[]{:S(2)}, u32[]{:S(2)}) async-start(f32[64,16,128]{2,0,1:T(8,128)} %copy.36), calls=%async_computation.2 | async-start | bytes 1048576 | tf_op jit(solution)/shard_map/all_to_all | solution.py:162
  100.4 3.3 %add_convert_fusion.1 = bf16[16,64,128]{2,1,0:T(8,128)(2,1)} fusion(f32[22,70,128]{2,1,0:T(8,128)S(1)} %get-tuple-element.11, bf16[16,64,128]{2,1,0:T(8,128)(2,1)S(1)} %copy-done.3, f32[3,18,66,128]{3,2,1,0:T(8,128)S(1)} %slice_convert_fusion), kind=kLoop, calls=%fused_computation.77 | loop fusion | flops 12845056 | bytes 9723904 | tf_op jit(solution)/shard_map/convert_element_type | solution.py:171
  103.6 9.8 %all-to-all-done.2 = f32[64,16,128]{2,0,1:T(8,128)S(1)} async-done(((f32[64,16,128]{2,0,1:T(8,128)}), f32[64,16,128]{2,0,1:T(8,128)S(1)}, u32[]{:S(2)}, u32[]{:S(2)}) %all-to-all-start.2) | async-done | bytes 524320 | tf_op jit(solution)/shard_map/all_to_all | solution.py:162
  113.5 2.6 %copy.37 = f32[16,64,1,128]{0,3,1,2:T(8,128)} copy(f32[16,64,1,128]{3,1,0,2:T(8,128)S(1)} %bitcast.152) | data formatting | bytes 1048576 | tf_op jit(solution)/shard_map/all_to_all | solution.py:162
  116.1 5.9 %convolution_bitcast_fusion.1 = f32[64,16,128]{2,1,0:T(8,128)S(1)} fusion(f32[16,64,8,16]{0,3,2,1:T(8,128)} %bitcast.144, f32[16,8]{0,1:T(8,128)S(1)} %fusion.64, s32[16,8]{0,1:T(8,128)S(1)} %add_select_fusion.3, pred[16,8]{0,1:T(8,128)(4,1)S(1)} %fusion.62), kind=kOutput, calls=%fused_computation.34 | convolution fusion | flops 201588736 | bytes 1049728 | tf_op jit(solution)/shard_map/gkmx,ygm->kxy/dot_general | solution.py:164
  123.4 2.4 %reshape.369 = f32[2,1,65536]{2,1,0:T(1,128)} reshape(f32[128,16,64]{2,1,0:T(8,128)} %bitcast.145) | data formatting | bytes 1048576
  125.8 3.8 %all-to-all-start.3 = ((f32[2,1,65536]{2,1,0:T(1,128)}), f32[2,1,65536]{2,1,0:T(1,128)S(1)}, u32[]{:S(2)}, u32[]{:S(2)}) async-start(f32[2,1,65536]{2,1,0:T(1,128)} %reshape.369), calls=%async_computation.3 | async-start | bytes 1048576 | tf_op jit(solution)/shard_map/all_to_all | solution.py:165
  129.6 4.1 %add_convert_fusion = bf16[16,64,128]{2,1,0:T(8,128)(2,1)} fusion(f32[22,70,128]{2,1,0:T(8,128)S(1)} %get-tuple-element.10, bf16[16,64,128]{2,1,0:T(8,128)(2,1)} %param.9, f32[3,18,66,128]{3,2,1,0:T(8,128)S(1)} %slice_convert_fusion), kind=kLoop, calls=%fused_computation.76 | loop fusion | flops 12845056 | bytes 9723904 | tf_op jit(solution)/shard_map/convert_element_type | solution.py:172
  137.7 2.2 %reduce.1 = f32[2,65536]{1,0:T(2,128)S(1)} reduce(f32[2,1,65536]{2,1,0:T(1,128)S(1)} %all-to-all-done.3, f32[]{:T(128)} %broadcast.801), dimensions={1}, to_apply=%all_to_all.58.reduce_sub_computation | reduce | bytes 1048580 | tf_op jit(solution)/shard_map/all_to_all | solution.py:165
  (64 shorter events, 38.0 us)
Async XLA Ops:
  0.6 4.0 %copy-start.4 = (bf16[16,64,128]{2,1,0:T(8,128)(2,1)S(1)}, bf16[16,64,128]{2,1,0:T(8,128)(2,1)}, u32[]{:S(2)}) copy-start(bf16[16,64,128]{2,1,0:T(8,128)(2,1)} %param.9) | copy-start | bytes 786436
  4.7 10.4 %collective-permute-start = (bf16[5,4,64,128]{3,2,1,0:T(8,128)(2,1)S(1)}, bf16[5,4,64,128]{3,2,1,0:T(8,128)(2,1)S(1)}, u32[]{:S(2)}, u32[]{:S(2)}) collective-permute-start(bf16[5,4,64,128]{3,2,1,0:T(8,128)(2,1)S(1)} %get-tuple-element.17), channel_id=1, source_target_pairs={{0,2},{2,4},{4,6},{6,8},{8,10},{10,12},{12,14},{14,16},{16,18},{18... | collective-permute-start | bytes 983048 | tf_op jit(solution)/shard_map/ppermute | solution.py:22
  5.2 9.9 %collective-permute-start.1 = (bf16[5,4,64,128]{3,2,1,0:T(8,128)(2,1)S(1)}, bf16[5,4,64,128]{3,2,1,0:T(8,128)(2,1)S(1)}, u32[]{:S(2)}, u32[]{:S(2)}) collective-permute-start(bf16[5,4,64,128]{3,2,1,0:T(8,128)(2,1)S(1)} %get-tuple-element.18), channel_id=1, source_target_pairs={{2,0},{4,2},{6,4},{8,6},{10,8},{12,10},{14,12},{16,14},{18,16},{20... | collective-permute-start | bytes 983048 | tf_op jit(solution)/shard_map/ppermute | solution.py:24
  15.2 4.9 %collective-permute-start.2 = (bf16[5,24,4,128]{3,2,1,0:T(4,128)(2,1)S(1)}, bf16[5,24,4,128]{3,2,1,0:T(4,128)(2,1)S(1)}, u32[]{:S(2)}, u32[]{:S(2)}) collective-permute-start(bf16[5,24,4,128]{3,2,1,0:T(4,128)(2,1)S(1)} %get-tuple-element.15), channel_id=1, source_target_pairs={{0,1},{1,0},{2,3},{3,2},{4,5},{5,4},{6,7},{7,6},{8,9},{9,8},{10,11... | collective-permute-start | bytes 368648 | tf_op jit(solution)/shard_map/ppermute | solution.py:22
  17.2 6.2 %collective-permute-start.3 = (bf16[5,24,4,128]{3,2,1,0:T(4,128)(2,1)S(1)}, bf16[5,24,4,128]{3,2,1,0:T(4,128)(2,1)S(1)}, u32[]{:S(2)}, u32[]{:S(2)}) collective-permute-start(bf16[5,24,4,128]{3,2,1,0:T(4,128)(2,1)S(1)} %get-tuple-element.16), channel_id=1, source_target_pairs={{1,0},{0,1},{3,2},{2,3},{5,4},{4,5},{7,6},{6,7},{9,8},{8,9},{11,10... | collective-permute-start | bytes 368648 | tf_op jit(solution)/shard_map/ppermute | solution.py:24
  25.7 1.4 copy-start
  34.0 4.3 %copy-start.1 = (f32[18,66,128]{2,1,0:T(8,128)}, f32[18,66,128]{2,1,0:T(8,128)S(1)}, u32[]{:S(2)}) copy-start(f32[18,66,128]{2,1,0:T(8,128)S(1)} %multiply_add_fusion) | copy-start | bytes 1824772
  37.1 1.3 copy-start.2
  43.1 12.8 %all-to-all-start = ((f32[2,1,65536]{2,1,0:T(1,128)}), f32[2,1,65536]{2,1,0:T(1,128)S(1)}, u32[]{:S(2)}, u32[]{:S(2)}) async-start(f32[2,1,65536]{2,1,0:T(1,128)} %reshape.367), calls=%async_computation | async-start | bytes 1048576 | tf_op jit(solution)/shard_map/all_to_all | solution.py:140
  67.7 18.5 %all-to-all-start.1 = ((f32[64,16,128]{2,0,1:T(8,128)}), f32[64,16,128]{2,0,1:T(8,128)S(1)}, u32[]{:S(2)}, u32[]{:S(2)}) async-start(f32[64,16,128]{2,0,1:T(8,128)} %copy.34), calls=%async_computation.1 | async-start | bytes 1048576 | tf_op jit(solution)/shard_map/all_to_all | solution.py:145
  94.9 18.6 %all-to-all-start.2 = ((f32[64,16,128]{2,0,1:T(8,128)}), f32[64,16,128]{2,0,1:T(8,128)S(1)}, u32[]{:S(2)}, u32[]{:S(2)}) async-start(f32[64,16,128]{2,0,1:T(8,128)} %copy.36), calls=%async_computation.2 | async-start | bytes 1048576 | tf_op jit(solution)/shard_map/all_to_all | solution.py:162
  99.0 1.4 copy-start.3
  125.8 11.9 %all-to-all-start.3 = ((f32[2,1,65536]{2,1,0:T(1,128)}), f32[2,1,65536]{2,1,0:T(1,128)S(1)}, u32[]{:S(2)}, u32[]{:S(2)}) async-start(f32[2,1,65536]{2,1,0:T(1,128)} %reshape.369), calls=%async_computation.3 | async-start | bytes 1048576 | tf_op jit(solution)/shard_map/all_to_all | solution.py:165
where the time goes:
time: 145 us; the launch traced here: 144 us
  waiting for transfers between devices  43.9 us (30%)
  local copies, waits for them, and re-layouts  29.6 us (20%)
  other arithmetic  28.7 us (20%)
  starting transfers between devices  23.2 us (16%)
  matrix products  17.2 us (12%)
    all_to_all x1, waiting for transfers between devices, body(): lax.all_to_all(packed, 'gx', split_axis=1, concat_axis=0, tiled=True)  14.2 us
    unnamed x19, local copies, waits for them, and re-layouts  11 us
    all_to_all x1, waiting for transfers between devices, body(): lax.all_to_all(back_x, 'gx', split_axis=1, concat_axis=0, tiled=True)  9.82 us
    all_to_all x1, waiting for transfers between devices, body(): lax.all_to_all(spectral_z, 'gy', split_axis=0, concat_axis=2, tiled=True)  8.75 us
    ppermute x2, waiting for transfers between devices, with_halo(): lax.ppermute(tail, axis, [(i, (i + 1) % count) for i in range(count)])  7.56 us
    add x2, other arithmetic, body(): starred.append(winds[position] + time_step * change)  6.07 us
    dot_general x1, matrix products, body(): jnp.einsum('gkmx,ygm->kxy', returned_x, table_yg, precision=highest)  5.88 us
    ppermute x2, starting transfers between devices, with_halo(): lax.ppermute(head, axis, [((i + 1) % count, i) for i in range(count)])  5.15 us
  transfers between devices with their start and end apart: 8, of which 7 were waited for; matrix products, arithmetic and copies ran while one was open for 9% of the time, Pallas kernels for 0%

commit v1 on v0

v1 whole, which is shorter than its diff:
```python
import functools
import math

import jax
import jax.numpy as jnp
import ml_dtypes
import numpy as np
from jax import lax
from jax.experimental import pallas as pl
from jax.experimental.pallas import tpu as pltpu
from jax.sharding import PartitionSpec as P

time_step = 0.25
diffusion = 0.1
f32 = jnp.float32
bf16 = jnp.bfloat16
MESH = pl.DeviceIdType.MESH


def split_table(table):
    high = table.astype(ml_dtypes.bfloat16)
    low = (table - high.astype(np.float64)).astype(ml_dtypes.bfloat16)
    return high, low


def cosine_table(length):
    grid = np.arange(length)[:, None]
    mode = np.arange(length)[None, :]
    scaling = np.where(mode == 0, math.sqrt(1.0 / length), math.sqrt(2.0 / length))
    return np.cos(math.pi / (2.0 * length) * (mode * (2 * grid + 1) % (4 * length))) * scaling


def fourier_table(length):
    grid = np.arange(length)[:, None]
    mode = np.arange(length)[None, :]
    half = length // 2
    freq = np.where(mode <= half, mode, mode - half)
    angle = 2.0 * math.pi / length * (grid * freq % length)
    scaling = np.where((mode == 0) | (mode == half), math.sqrt(1.0 / length), math.sqrt(2.0 / length))
    return np.where(mode <= half, np.cos(angle), np.sin(angle)) * scaling


def make_tables(D, G, XL, YL, Z):
    N, Y, KB, XP = D * XL, G * YL, Z // G, XL // G
    cz = cosine_table(Z)
    full = np.zeros((G, Z, G, G, KB))
    for g in range(G):
        for h in range(G):
            full[h, :, g, h, :] = cz[:, g * KB : (g + 1) * KB]
    full = full.reshape(G * Z, G * Z)
    mode = np.arange(Y)
    freq = np.where(mode <= Y // 2, mode, mode - Y // 2)
    eig_y = 2.0 * np.cos(2.0 * math.pi / Y * freq) - 2.0
    eig_z = 2.0 * np.cos(math.pi / Z * np.arange(Z)) - 2.0
    half_b = 1.0 - 0.5 * (eig_z[:, None] + eig_y[None, :])
    half_b[0, 0] = 2.0
    q = np.exp(-np.arccosh(half_b))
    factor = -q / (1.0 - q * q)
    q[0, 0] = 0.0
    factor[0, 0] = 0.0
    jump = q**XL
    wrap = 1.0 / (1.0 - q**N)
    ch = 2 * KB * Y // (128 * D)

    def tiles(table):
        blocks = []
        for g in range(G):
            rows = table[g * KB : (g + 1) * KB]
            part = [
                rows[k : k + ch, c : c + 128] for c in range(0, Y, 128) for k in range(0, KB, ch)
            ]
            blocks.append(np.stack(part + part))
        return np.stack(blocks).astype(np.float32)

    dist = np.arange(N)
    green = dist / 2.0 - dist * dist / (2.0 * N)
    green = green - green.mean()
    spot = (np.arange(N)[None, None, :] - XL * np.arange(D)[:, None, None] - np.arange(XL)[None, :, None]) % N
    z = np.arange(Z)
    band = np.zeros((Z, 3 * Z))
    for offset, c, d in zip(range(-3, 4), (-1, 9, -45, 0, 45, -9, 1), (1, -6, 15, -20, 15, -6, 1)):
        for k in range(Z):
            if 0 <= k + offset < Z:
                band[k + offset, k] = c
                band[k + offset, Z + k] = d
                if abs(offset) == 1:
                    band[k + offset, 2 * Z + k] = 1.0
    return (
        band.astype(ml_dtypes.bfloat16),
        *split_table(full),
        *split_table(fourier_table(Y)),
        q.reshape(G, KB, Y).astype(np.float32),
        factor.reshape(G, KB, Y).astype(np.float32),
        tiles(jump),
        tiles(wrap),
        green[spot].astype(np.float32),
    )


def two(value):
    high = value.astype(bf16)
    return high, (value - high.astype(f32)).astype(bf16)


def dot(a, b):
    return jnp.dot(a, b, preferred_element_type=f32)


def dot_nt(a, b):
    return lax.dot_general(a, b, (((1,), (1,)), ((), ())), preferred_element_type=f32)


def kernel(D, G, XL, YL, Z, *refs):
    (vx, vy, vz, temp, water, band, full_h, full_l, four_h, four_l, q_ref, fac_ref, jump, wrap, green,
     out_x, out_y, out_z, out_t, out_w, out_p,
     pad, zbuf, edge, ysend, xhalo, yhalo, corner, sx, sy, src,
     snd, got, spec, ends, ends_in, carry, carry_in, cplane, back, back_in,
     halo_send, halo_recv, gy_send, gy_recv, end_send, end_recv, car_send, car_recv, ret_send, ret_recv) = refs
    fields = (vx, vy, vz, temp, water)
    N, Y, KB, XP = D * XL, G * YL, Z // G, XL // G
    ch = carry.shape[1]
    H = D // 2
    ix, iy = lax.axis_index("gx"), lax.axis_index("gy")
    right, left = lax.rem(ix + 1, D), lax.rem(ix + D - 1, D)
    above, below = lax.rem(iy + 1, G), lax.rem(iy + G - 1, G)
    gx_peers = [lax.rem(ix + step, D) for step in range(1, D)]
    gy_peers = [lax.rem(iy + step, G) for step in range(1, G)]

    barrier = pltpu.get_barrier_semaphore()
    known = [(peer, iy) for peer in gx_peers] + [(ix, peer) for peer in gy_peers]
    known += [(right, above), (right, below), (left, above), (left, below)]
    for device in known:
        pl.semaphore_signal(barrier, inc=1, device_id=device, device_id_type=MESH)

    for f in range(5):
        for x in range(XL):
            edge[0, f, 4 * x : 4 * x + 4, :] = fields[f][x, 0:16, :].astype(f32)[0:4]
            edge[1, f, 4 * x : 4 * x + 4, :] = fields[f][x, YL - 16 : YL, :].astype(f32)[12:16]
    ysend[...] = edge[...].astype(bf16)
    pl.semaphore_wait(barrier, len(known))

    def remote(src_ref, dst_ref, send, recv, device):
        copy = pltpu.make_async_remote_copy(
            src_ref=src_ref, dst_ref=dst_ref, send_sem=send, recv_sem=recv,
            device_id=device, device_id_type=MESH,
        )
        copy.start()
        return copy

    halos = []

    def halo(src_ref, dst_ref, device):
        slot = len(halos)
        halos.append(remote(src_ref, dst_ref, halo_send.at[slot], halo_recv.at[slot], device))

    lines = 4 * XL
    for f in range(5):
        halo(fields[f].at[XL - 4 : XL], xhalo.at[0, f], (right, iy))
        halo(fields[f].at[0:4], xhalo.at[1, f], (left, iy))
    halo(ysend.at[1], yhalo.at[0], (ix, above))
    halo(ysend.at[0], yhalo.at[1], (ix, below))
    halo(ysend.at[1, :, lines - 16 : lines], corner.at[0], (right, above))
    halo(ysend.at[0, :, lines - 16 : lines], corner.at[1], (right, below))
    halo(ysend.at[1, :, 0:16], corner.at[2], (left, above))
    halo(ysend.at[0, :, 0:16], corner.at[3], (left, below))

    for f in range(5):
        pad[f, :, 0:8, :] = jnp.zeros((XL + 8, 8, Z), f32)
        pad[f, :, YL + 8 : YL + 16, :] = jnp.zeros((XL + 8, 8, Z), f32)
        pad[f, 4 : XL + 4, 8 : YL + 8, :] = fields[f][...].astype(f32)
    for copy in halos:
        copy.wait()
    for f in range(5):
        pad[f, 0:4, 8 : YL + 8, :] = xhalo[0, f].astype(f32)
        pad[f, XL + 4 : XL + 8, 8 : YL + 8, :] = xhalo[1, f].astype(f32)
        for side, row in ((0, 4), (1, YL + 8)):
            strip = yhalo[side, f].astype(f32)
            for x in range(XL):
                pad[f, 4 + x, row : row + 4, :] = strip[4 * x : 4 * x + 4]
            for far, start in ((0, 0), (2, XL + 4)):
                strip_c = corner[far + side, f].astype(f32)
                for x in range(4):
                    pad[f, start + x, row : row + 4, :] = strip_c[4 * x : 4 * x + 4]

    group = (XL + 8) // 4

    def along_z(f):
        def step(i, _):
            planes = pad[f, pl.ds(i * group, group)]
            rows = planes.reshape(group * (YL + 16), Z).astype(bf16)
            zbuf[pl.ds(i * group, group)] = dot(rows, band[...]).reshape(group, YL + 16, 3 * Z)
            return 0

        lax.fori_loop(0, 4, step, 0)

    def star(f, px, start, rows):
        low = 8 + start
        here = pl.ds(low, rows)
        centre = pad[f, px, here, :]
        sums = zbuf[px, here, 2 * Z : 3 * Z]
        speed = pad[2, px, here, :]
        total = speed * zbuf[px, here, 0:Z] - jnp.abs(speed) * zbuf[px, here, Z : 2 * Z]
        for axis in range(2):
            if axis == 0:
                get = lambda s: pad[f, px + s, here, :]
            else:
                get = lambda s: pad[f, px, pl.ds(low + s, rows), :]
            m1, p1, m2, p2, m3, p3 = get(-1), get(1), get(-2), get(2), get(-3), get(3)
            one = m1 + p1
            central = 45.0 * (p1 - m1) - 9.0 * (p2 - m2) + (p3 - m3)
            damped = 15.0 * one - 6.0 * (m2 + p2) + (m3 + p3) - 20.0 * centre
            speed = pad[axis, px, here, :]
            total = total + (speed * central - jnp.abs(speed) * damped)
            sums = sums + one
        result = centre + (time_step * diffusion) * (sums - 6.0 * centre) - (time_step / 60.0) * total
        if f == 2:
            result = result + time_step * pad[3, px, here, :]
        return result

    along_z(0)

    def step_x(x, _):
        for start in range(0, YL, 16):
            sx[x, start : start + 16, :] = star(0, x + 3, start, 16)
        return 0

    lax.fori_loop(0, XL + 2, step_x, 0)
    along_z(1)

    def step_y(x, _):
        for start in range(-1, YL - 16, 16):
            sy[x, start + 8 : start + 24, :] = star(1, x + 4, start, 16)
        sy[x, YL + 1 : YL + 9, :] = star(1, x + 4, YL - 7, 8)
        return 0

    lax.fori_loop(0, XL, step_y, 0)
    along_z(2)
    lane = lax.broadcasted_iota(jnp.int32, (16, Z), 1)

    def step_z(x, _):
        for start in range(0, YL, 16):
            here = pl.ds(start, 16)
            value = star(2, x + 4, start, 16)
            out_z[x, here, :] = value.astype(bf16)
            out_x[x, here, :] = sx[x + 1, here, :].astype(bf16)
            out_y[x, here, :] = sy[x, pl.ds(start + 8, 16), :].astype(bf16)
            up = jnp.where(lane < Z - 1, pltpu.roll(value, Z - 1, 1), 0.0)
            down = jnp.where(lane > 0, pltpu.roll(value, 1, 1), 0.0)
            grad = (sx[x + 2, here, :] - sx[x, here, :]) + (up - down)
            grad = grad + (sy[x, pl.ds(start + 9, 16), :] - sy[x, pl.ds(start + 7, 16), :])
            src[x, here, :] = grad * (0.5 / time_step)
        return 0

    lax.fori_loop(0, XL, step_z, 0)

    lhs = [two(src[h * XP : (h + 1) * XP].reshape(XP * YL, Z)) for h in range(G)]
    for g in range(G):
        cols = slice(g * Z, (g + 1) * Z)
        part = jnp.zeros((XP * YL, Z), f32)
        for h in range(G):
            rows = slice(h * Z, (h + 1) * Z)
            high, low = lhs[h]
            part = part + dot(high, full_h[rows, cols]) + dot(high, full_l[rows, cols]) + dot(low, full_h[rows, cols])
        snd[g] = part.reshape(XP, YL, Z)
    mine = pl.ds(pl.multiple_of(iy * YL, YL), YL)
    copies = [
        remote(snd.at[peer], got.at[:, mine, :], gy_send.at[n], gy_recv.at[n], (ix, peer))
        for n, peer in enumerate(gy_peers)
    ]
    got[:, mine, :] = snd[iy]

    for f, target in ((3, out_t), (4, out_w)):
        along_z(f)

        def step_s(x, _):
            for start in range(0, YL, 16):
                target[x, start : start + 16, :] = star(f, x + 4, start, 16).astype(bf16)
            return 0

        lax.fori_loop(0, XL, step_s, 0)
    for copy in copies:
        copy.wait()

    def fourier(i, _):
        high, low = two(got[i].T)
        spec[i] = dot(high, four_h[...]) + dot(high, four_l[...]) + dot(low, four_h[...])
        return 0

    lax.fori_loop(0, XP, fourier, 0)

    def line(x):
        h, i = x // XP, x % XP
        return i, slice(h * KB, (h + 1) * KB)

    q = q_ref[iy]
    end_a = spec[line(0)]
    for x in range(1, XL):
        end_a = spec[line(x)] + q * end_a
    end_b = spec[line(XL - 1)]
    for x in range(XL - 2, -1, -1):
        end_b = spec[line(x)] + q * end_b
    share = jnp.zeros((1, N), f32)
    for x in range(XL):
        i, rows = line(x)
        share = share + spec[i, rows.start : rows.start + 1, 0:1] * green[ix, x : x + 1, :]
    row8 = lax.broadcasted_iota(jnp.int32, (8, 128), 0)
    extra = jnp.zeros((8, 128), f32)
    for r in range(N // 128):
        extra = extra + jnp.where(row8 == r, share[:, r * 128 : (r + 1) * 128], 0.0)
    blocks = [(c, k) for c in range(0, Y, 128) for k in range(0, KB, ch)]
    for n, (c, k) in enumerate(blocks):
        ends[n, 0:ch, :] = end_a[k : k + ch, c : c + 128]
        ends[H + n, 0:ch, :] = end_b[k : k + ch, c : c + 128]
    for n in range(D):
        if ch < 8:
            ends[n, ch:8, :] = jnp.zeros((8 - ch, 128), f32)
        ends[n, 8:16, :] = extra

    def slot_of(device, worker):
        return device + (worker // H) * (D - 1 - 2 * device)

    copies = []
    for n, peer in enumerate(gx_peers):
        copies.append(
            remote(ends.at[peer], ends_in.at[slot_of(ix, peer)], end_send.at[n], end_recv.at[n], (peer, iy))
        )
    ends_in[slot_of(ix, ix)] = ends[ix]
    for copy in copies:
        copy.wait()
    jump_t, wrap_t = jump[iy, ix], wrap[iy, ix]
    state = ends_in[0, 0:ch, :]
    whole = ends_in[0, 8:16, :]
    for s in range(1, D):
        state = ends_in[s, 0:ch, :] + jump_t * state
        whole = whole + ends_in[s, 8:16, :]
    state = state * wrap_t
    for s in range(D):
        carry[s] = state
        if s < D - 1:
            state = ends_in[s, 0:ch, :] + jump_t * state
    copies = []
    for n, peer in enumerate(gx_peers):
        copies.append(
            remote(carry.at[slot_of(peer, ix)], carry_in.at[ix], car_send.at[n], car_recv.at[n], (peer, iy))
        )
    carry_in[ix] = carry[slot_of(ix, ix)]
    column = jnp.zeros((XL, 1), f32)
    for r in range(N // 128):
        spot = lax.broadcasted_iota(jnp.int32, (XL, 128), 1) + r * 128
        want = lax.broadcasted_iota(jnp.int32, (XL, 128), 0) + ix * XL
        column = column + jnp.sum(jnp.where(spot == want, whole[r : r + 1, :], 0.0), axis=1, keepdims=True)
    first = (lax.broadcasted_iota(jnp.int32, (XL, 128), 1) + iy) == 0
    column = jnp.where(first, column, 0.0)
    for copy in copies:
        copy.wait()
    for n, (c, k) in enumerate(blocks):
        cplane[0, k : k + ch, c : c + 128] = carry_in[n]
        cplane[1, k : k + ch, c : c + 128] = carry_in[H + n]
    factor = fac_ref[iy]
    state = cplane[0]
    for x in range(XL):
        i, rows = line(x)
        state = spec[i, rows, :] + q * state
        snd_i = pl.ds(0, KB)
        back[x, snd_i, :] = state
    state = cplane[1]
    for x in range(XL - 1, -1, -1):
        i, rows = line(x)
        value = spec[i, rows, :]
        ahead = q * state
        state = value + ahead
        spec[i, rows, :] = factor * (back[x, 0:KB, :] + ahead)
        spec[i, rows.start : rows.start + 1, 0:128] += column[x : x + 1, :]

    slabs = got

    def unfourier(i, _):
        high, low = two(spec[i])
        slabs[i] = dot_nt(four_h[...], high) + dot_nt(four_h[...], low) + dot_nt(four_l[...], high)
        return 0

    lax.fori_loop(0, XP, unfourier, 0)
    copies = []
    for n, peer in enumerate(gy_peers):
        part = pl.ds(pl.multiple_of(peer * YL, YL), YL)
        copies.append(
            remote(slabs.at[:, part, :], back_in.at[iy], ret_send.at[n], ret_recv.at[n], (ix, peer))
        )
    back_in[iy] = slabs[:, mine, :]
    for copy in copies:
        copy.wait()
    rhs = [two(back_in[g].reshape(XP * YL, Z)) for g in range(G)]
    for h in range(G):
        rows = slice(h * Z, (h + 1) * Z)
        part = jnp.zeros((XP * YL, Z), f32)
        for g in range(G):
            cols = slice(g * Z, (g + 1) * Z)
            high, low = rhs[g]
            part = part + dot_nt(high, full_h[rows, cols]) + dot_nt(high, full_l[rows, cols]) + dot_nt(low, full_h[rows, cols])
        out_p[h * XP : (h + 1) * XP] = part.reshape(XP, YL, Z)


def body(D, G, velocity_x, velocity_y, velocity_z, potential_temp, total_water):
    XL, YL, Z = velocity_x.shape
    Y, KB, XP = G * YL, Z // G, XL // G
    ch = 2 * KB * Y // (128 * D)
    tables = [jnp.asarray(t) for t in make_tables(D, G, XL, YL, Z)]
    dma = pltpu.SemaphoreType.DMA
    V = pltpu.VMEM
    scratch = [
        V((5, XL + 8, YL + 16, Z), f32),
        V((XL + 8, YL + 16, 3 * Z), f32),
        V((2, 5, 4 * XL, Z), f32),
        V((2, 5, 4 * XL, Z), bf16),
        V((2, 5, 4, YL, Z), bf16),
        V((2, 5, 4 * XL, Z), bf16),
        V((4, 5, 16, Z), bf16),
        V((XL + 2, YL, Z), f32),
        V((XL, YL + 16, Z), f32),
        V((XL, YL, Z), f32),
        V((G, XP, YL, Z), f32),
        V((XP, Y, Z), f32),
        V((XP, Z, Y), f32),
        V((D, 16, 128), f32),
        V((D, 16, 128), f32),
        V((D, ch, 128), f32),
        V((D, ch, 128), f32),
        V((2, KB, Y), f32),
        V((XL, KB, Y), f32),
        V((G, XP, YL, Z), f32),
        dma((16,)), dma((16,)),
        dma((G,)), dma((G,)),
        dma((D,)), dma((D,)),
        dma((D,)), dma((D,)),
        dma((G,)), dma((G,)),
    ]
    block = jax.ShapeDtypeStruct((XL, YL, Z), bf16)
    vmem = pl.BlockSpec(memory_space=pltpu.VMEM)
    return pl.pallas_call(
        functools.partial(kernel, D, G, XL, YL, Z),
        out_shape=(block,) * 5 + (jax.ShapeDtypeStruct((XL, YL, Z), f32),),
        in_specs=[vmem] * (5 + len(tables)),
        out_specs=(vmem,) * 6,
        scratch_shapes=scratch,
        compiler_params=pltpu.CompilerParams(
            collective_id=0, has_side_effects=True, vmem_limit_bytes=56 * 1024 * 1024
        ),
    )(velocity_x, velocity_y, velocity_z, potential_temp, total_water, *tables)


def solution(mesh):
    spec = P("gx", "gy", None)
    return jax.shard_map(
        functools.partial(body, mesh.shape["gx"], mesh.shape["gy"]),
        mesh=mesh,
        in_specs=(spec,) * 5,
        out_specs=(spec,) * 6,
        check_vma=False,
    )
```

time: 145 us -> 61 us (0.42)
  Pallas kernels: 0 us -> 54.1 us
  waiting for transfers between devices: 43.9 us -> 0 us
  other arithmetic: 28.7 us -> 0 us
  local copies, waits for them, and re-layouts: 29.6 us -> 6.01 us
  starting transfers between devices: 23.2 us -> 0 us
  matrix products: 17.2 us -> 0 us
    pallas_call x0 -> x1, Pallas kernels: none -> 54.1 us  [body(): pl.pallas_call(functools.partial(kernel, D, G, XL, YL, Z), out_shape=(blo...]
    all_to_all x4 -> x0, waiting for transfers between devices: 33.1 us -> none  [the longest x1 14.2 us: body(): lax.all_to_all(packed, 'gx', split_axis=1, concat_axis=0, tiled=True)]
    dot_general x6 -> x0, matrix products: 17.2 us -> none  [the longest x1 5.88 us: body(): jnp.einsum('gkmx,ygm->kxy', returned_x, table_yg, precision=highest)]
    all_to_all x4 -> x0, starting transfers between devices: 15.6 us -> none  [the longest x1 4.11 us: body(): lax.all_to_all(back_x, 'gx', split_axis=1, concat_axis=0, tiled=True)]
    ppermute x4 -> x0, waiting for transfers between devices: 10.8 us -> none  [the longest x2 7.56 us: with_halo(): lax.ppermute(tail, axis, [(i, (i + 1) % count) for i in range(count)])]
    convert_element_type x6 -> x0, other arithmetic: 10.5 us -> none  [the longest x1 4.14 us: body(): scalars[1].astype(jnp.bfloat16)]
    all_to_all x7 -> x0, local copies, waits for them, and re-layouts: 9.47 us -> none  [the longest x3 4.13 us: body(): lax.all_to_all(spectral_z, 'gy', split_axis=0, concat_axis=2, tiled=True)]
    ppermute x4 -> x0, starting transfers between devices: 7.65 us -> none  [the longest x2 5.15 us: with_halo(): lax.ppermute(head, axis, [((i + 1) % count, i) for i in range(count)])]
  transfers between devices with their start and end apart: 8 -> 0, of which waited for: 7 -> 0; matrix products, arithmetic and copies ran while one was open for 9% -> 0% of each run, Pallas kernels for 0% -> 0%
where the time goes in v1:
time: 61 us; the launch traced here: 60.8 us
  Pallas kernels  54.1 us (89%)
  local copies, waits for them, and re-layouts  6.01 us (10%)
  between operations  0.66 us (1%)
    pallas_call x1, Pallas kernels, body(): pl.pallas_call(functools.partial(kernel, D, G, XL, YL, Z), out_shape=(blo...  54.1 us
    unnamed x16, local copies, waits for them, and re-layouts  6.01 us

profile of v1, /device:TPU:0, one launch (start us, length us, event | category | flops | bytes accessed | tf_op | source)
XLA Modules:
  0.0 60.8 jit_solution(5204265826017765143)
XLA Ops:
  0.6 54.1 %shard_map.190 = (bf16[16,64,128]{2,1,0:T(8,128)(2,1)}, bf16[16,64,128]{2,1,0:T(8,128)(2,1)}, bf16[16,64,128]{2,1,0:T(8,128)(2,1)}, bf16[16,64,128]{2,1,0:T(8,12...) custom-call(bf16[16,64,128]{2,1,0:T(8,128)(2,1)} %refs_0_.1, bf16[16,64,128]{2,1,0:T(8,128)(2,1)} %refs_1_.1, ...), custom_call_target="tpu_custom_call" | custom-call | tf_op jit(solution)/shard_map/pallas_call | solution.py:439
  54.8 0.0 copy-start.4
  54.8 1.7 %copy.27 = bf16[16,64,128]{2,1,0:T(8,128)(2,1)} copy(bf16[16,64,128]{2,1,0:T(8,128)(2,1)} %get-tuple-element.12) | data formatting | bytes 524288
  56.5 0.0 copy-done.4
  56.5 0.0 copy-start.3
  56.5 0.7 %copy.28 = bf16[16,64,128]{2,1,0:T(8,128)(2,1)} copy(bf16[16,64,128]{2,1,0:T(8,128)(2,1)S(1)} %copy-done.4) | data formatting | bytes 524288
  57.2 0.3 copy-done.3
  57.5 0.0 copy-start.2
  57.5 0.0 copy-start.1
  57.5 0.7 %copy.29 = bf16[16,64,128]{2,1,0:T(8,128)(2,1)} copy(bf16[16,64,128]{2,1,0:T(8,128)(2,1)S(1)} %copy-done.3) | data formatting | bytes 524288
  58.2 0.3 copy-done.2
  58.6 0.0 copy-start
  58.6 0.7 %copy.30 = bf16[16,64,128]{2,1,0:T(8,128)(2,1)} copy(bf16[16,64,128]{2,1,0:T(8,128)(2,1)S(1)} %copy-done.2) | data formatting | bytes 524288
  59.3 0.0 copy-done.1
  59.3 0.7 %copy.31 = bf16[16,64,128]{2,1,0:T(8,128)(2,1)} copy(bf16[16,64,128]{2,1,0:T(8,128)(2,1)S(1)} %copy-done.1) | data formatting | bytes 524288
  60.0 0.0 copy-done
  60.0 0.8 %copy.32 = f32[16,64,128]{2,1,0:T(8,128)} copy(f32[16,64,128]{2,1,0:T(8,128)S(1)} %copy-done) | data formatting | bytes 1048576
Async XLA Ops:
  54.8 1.7 %copy-start.4 = (bf16[16,64,128]{2,1,0:T(8,128)(2,1)S(1)}, bf16[16,64,128]{2,1,0:T(8,128)(2,1)}, u32[]{:S(2)}) copy-start(bf16[16,64,128]{2,1,0:T(8,128)(2,1)} %get-tuple-element.13) | copy-start | bytes 786436
  56.5 1.0 %copy-start.3 = (bf16[16,64,128]{2,1,0:T(8,128)(2,1)S(1)}, bf16[16,64,128]{2,1,0:T(8,128)(2,1)}, u32[]{:S(2)}) copy-start(bf16[16,64,128]{2,1,0:T(8,128)(2,1)} %get-tuple-element.14) | copy-start | bytes 786436
  57.5 1.0 %copy-start.2 = (bf16[16,64,128]{2,1,0:T(8,128)(2,1)S(1)}, bf16[16,64,128]{2,1,0:T(8,128)(2,1)}, u32[]{:S(2)}) copy-start(bf16[16,64,128]{2,1,0:T(8,128)(2,1)} %get-tuple-element.15) | copy-start | bytes 786436
  57.5 1.7 %copy-start.1 = (bf16[16,64,128]{2,1,0:T(8,128)(2,1)S(1)}, bf16[16,64,128]{2,1,0:T(8,128)(2,1)}, u32[]{:S(2)}) copy-start(bf16[16,64,128]{2,1,0:T(8,128)(2,1)} %get-tuple-element.16) | copy-start | bytes 786436
  58.6 1.4 %copy-start = (f32[16,64,128]{2,1,0:T(8,128)S(1)}, f32[16,64,128]{2,1,0:T(8,128)}, u32[]{:S(2)}) copy-start(f32[16,64,128]{2,1,0:T(8,128)} %get-tuple-element.17) | copy-start | bytes 1572868

commit v2 on v1

--- a/solution.py
+++ b/solution.py
@@ -112,10 +112,10 @@
 
 def kernel(D, G, XL, YL, Z, *refs):
     (vx, vy, vz, temp, water, band, full_h, full_l, four_h, four_l, q_ref, fac_ref, jump, wrap, green,
-     out_x, out_y, out_z, out_t, out_w, out_p,
+     out_x, out_y, out_z, out_t, out_w, back_in,
      pad, zbuf, edge, ysend, xhalo, yhalo, corner, sx, sy, src,
-     snd, got, spec, ends, ends_in, carry, carry_in, cplane, back, back_in,
-     halo_send, halo_recv, gy_send, gy_recv, end_send, end_recv, car_send, car_recv, ret_send, ret_recv) = refs
+     snd, got, spec, ends, ends_in, extra_out, extra_in, carry, carry_in, cplane, back,
+     halo_send, halo_recv, gy_send, gy_recv, end_send, end_recv, ext_send, ext_recv, car_send, car_recv, ret_send, ret_recv) = refs
     fields = (vx, vy, vz, temp, water)
     N, Y, KB, XP = D * XL, G * YL, Z // G, XL // G
     ch = carry.shape[1]
@@ -168,6 +168,13 @@
         pad[f, :, 0:8, :] = jnp.zeros((XL + 8, 8, Z), f32)
         pad[f, :, YL + 8 : YL + 16, :] = jnp.zeros((XL + 8, 8, Z), f32)
         pad[f, 4 : XL + 4, 8 : YL + 8, :] = fields[f][...].astype(f32)
+
+        def along_z(i, _):
+            rows = fields[f][pl.ds(i * 4, 4)].reshape(4 * YL, Z)
+            zbuf[f, pl.ds(4 + i * 4, 4), 8 : YL + 8, :] = dot(rows, band[...]).reshape(4, YL, 3 * Z)
+            return 0
+
+        lax.fori_loop(0, XL // 4, along_z, 0)
     for copy in halos:
         copy.wait()
     for f in range(5):
@@ -182,24 +189,21 @@
                 for x in range(4):
                     pad[f, start + x, row : row + 4, :] = strip_c[4 * x : 4 * x + 4]
 
-    group = (XL + 8) // 4
-
-    def along_z(f):
-        def step(i, _):
-            planes = pad[f, pl.ds(i * group, group)]
-            rows = planes.reshape(group * (YL + 16), Z).astype(bf16)
-            zbuf[pl.ds(i * group, group)] = dot(rows, band[...]).reshape(group, YL + 16, 3 * Z)
-            return 0
-
-        lax.fori_loop(0, 4, step, 0)
+    outer = jnp.concatenate([pad[0, 3, 8 : YL + 8, :], pad[0, XL + 4, 8 : YL + 8, :]], axis=0)
+    outer = dot(outer.astype(bf16), band[...])
+    zbuf[0, 3, 8 : YL + 8, :] = outer[0:YL]
+    zbuf[0, XL + 4, 8 : YL + 8, :] = outer[YL:]
+    for row in (0, YL + 8):
+        outer = pad[1, 4 : XL + 4, row : row + 8, :].reshape(XL * 8, Z)
+        zbuf[1, 4 : XL + 4, row : row + 8, :] = dot(outer.astype(bf16), band[...]).reshape(XL, 8, 3 * Z)
 
     def star(f, px, start, rows):
         low = 8 + start
         here = pl.ds(low, rows)
         centre = pad[f, px, here, :]
-        sums = zbuf[px, here, 2 * Z : 3 * Z]
+        sums = zbuf[f, px, here, 2 * Z : 3 * Z]
         speed = pad[2, px, here, :]
-        total = speed * zbuf[px, here, 0:Z] - jnp.abs(speed) * zbuf[px, here, Z : 2 * Z]
+        total = speed * zbuf[f, px, here, 0:Z] - jnp.abs(speed) * zbuf[f, px, here, Z : 2 * Z]
         for axis in range(2):
             if axis == 0:
                 get = lambda s: pad[f, px + s, here, :]
@@ -217,15 +221,12 @@
             result = result + time_step * pad[3, px, here, :]
         return result
 
-    along_z(0)
-
     def step_x(x, _):
         for start in range(0, YL, 16):
             sx[x, start : start + 16, :] = star(0, x + 3, start, 16)
         return 0
 
     lax.fori_loop(0, XL + 2, step_x, 0)
-    along_z(1)
 
     def step_y(x, _):
         for start in range(-1, YL - 16, 16):
@@ -234,7 +235,6 @@
         return 0
 
     lax.fori_loop(0, XL, step_y, 0)
-    along_z(2)
     lane = lax.broadcasted_iota(jnp.int32, (16, Z), 1)
 
     def step_z(x, _):
@@ -253,40 +253,45 @@
 
     lax.fori_loop(0, XL, step_z, 0)
 
-    lhs = [two(src[h * XP : (h + 1) * XP].reshape(XP * YL, Z)) for h in range(G)]
-    for g in range(G):
-        cols = slice(g * Z, (g + 1) * Z)
-        part = jnp.zeros((XP * YL, Z), f32)
-        for h in range(G):
-            rows = slice(h * Z, (h + 1) * Z)
-            high, low = lhs[h]
-            part = part + dot(high, full_h[rows, cols]) + dot(high, full_l[rows, cols]) + dot(low, full_h[rows, cols])
-        snd[g] = part.reshape(XP, YL, Z)
     mine = pl.ds(pl.multiple_of(iy * YL, YL), YL)
-    copies = [
-        remote(snd.at[peer], got.at[:, mine, :], gy_send.at[n], gy_recv.at[n], (ix, peer))
-        for n, peer in enumerate(gy_peers)
-    ]
-    got[:, mine, :] = snd[iy]
-
-    for f, target in ((3, out_t), (4, out_w)):
-        along_z(f)
-
+    half = XP // 2
+    copies = []
+    for c in range(2):
+        planes = slice(c * half, (c + 1) * half)
+        lhs = [two(src[h * XP + c * half : h * XP + (c + 1) * half].reshape(half * YL, Z)) for h in range(G)]
+        for g in range(G):
+            cols = slice(g * Z, (g + 1) * Z)
+            part = jnp.zeros((half * YL, Z), f32)
+            for h in range(G):
+                rows = slice(h * Z, (h + 1) * Z)
+                high, low = lhs[h]
+                part = part + dot(high, full_h[rows, cols]) + dot(high, full_l[rows, cols]) + dot(low, full_h[rows, cols])
+            snd[g, planes] = part.reshape(half, YL, Z)
+        copies.append([
+            remote(snd.at[peer, planes], got.at[planes, mine, :], gy_send.at[c * G + n], gy_recv.at[c * G + n], (ix, peer))
+            for n, peer in enumerate(gy_peers)
+        ])
+        got[planes, mine, :] = snd[iy, planes]
+
+    def scalar(f, target, first, last):
         def step_s(x, _):
             for start in range(0, YL, 16):
                 target[x, start : start + 16, :] = star(f, x + 4, start, 16).astype(bf16)
             return 0
 
-        lax.fori_loop(0, XL, step_s, 0)
-    for copy in copies:
-        copy.wait()
+        lax.fori_loop(first, last, step_s, 0)
+
+    scalar(3, out_t, 0, XL)
 
     def fourier(i, _):
         high, low = two(got[i].T)
         spec[i] = dot(high, four_h[...]) + dot(high, four_l[...]) + dot(low, four_h[...])
         return 0
 
-    lax.fori_loop(0, XP, fourier, 0)
+    for c in range(2):
+        for copy in copies[c]:
+            copy.wait()
+        lax.fori_loop(c * half, (c + 1) * half, fourier, 0)
 
     def line(x):
         h, i = x // XP, x % XP
@@ -309,12 +314,9 @@
         extra = extra + jnp.where(row8 == r, share[:, r * 128 : (r + 1) * 128], 0.0)
     blocks = [(c, k) for c in range(0, Y, 128) for k in range(0, KB, ch)]
     for n, (c, k) in enumerate(blocks):
-        ends[n, 0:ch, :] = end_a[k : k + ch, c : c + 128]
-        ends[H + n, 0:ch, :] = end_b[k : k + ch, c : c + 128]
-    for n in range(D):
-        if ch < 8:
-            ends[n, ch:8, :] = jnp.zeros((8 - ch, 128), f32)
-        ends[n, 8:16, :] = extra
+        ends[n] = end_a[k : k + ch, c : c + 128]
+        ends[H + n] = end_b[k : k + ch, c : c + 128]
+    extra_out[...] = extra
 
     def slot_of(device, worker):
         return device + (worker // H) * (D - 1 - 2 * device)
@@ -324,26 +326,35 @@
         copies.append(
             remote(ends.at[peer], ends_in.at[slot_of(ix, peer)], end_send.at[n], end_recv.at[n], (peer, iy))
         )
+    extras = []
+    for n, peer in enumerate(gx_peers):
+        extras.append(remote(extra_out, extra_in.at[ix], ext_send.at[n], ext_recv.at[n], (peer, iy)))
+    extra_in[ix] = extra
     ends_in[slot_of(ix, ix)] = ends[ix]
+    scalar(4, out_w, 0, XL // 2)
     for copy in copies:
         copy.wait()
     jump_t, wrap_t = jump[iy, ix], wrap[iy, ix]
-    state = ends_in[0, 0:ch, :]
-    whole = ends_in[0, 8:16, :]
+    state = ends_in[0]
     for s in range(1, D):
-        state = ends_in[s, 0:ch, :] + jump_t * state
-        whole = whole + ends_in[s, 8:16, :]
+        state = ends_in[s] + jump_t * state
     state = state * wrap_t
     for s in range(D):
         carry[s] = state
         if s < D - 1:
-            state = ends_in[s, 0:ch, :] + jump_t * state
+            state = ends_in[s] + jump_t * state
     copies = []
     for n, peer in enumerate(gx_peers):
         copies.append(
             remote(carry.at[slot_of(peer, ix)], carry_in.at[ix], car_send.at[n], car_recv.at[n], (peer, iy))
         )
     carry_in[ix] = carry[slot_of(ix, ix)]
+    scalar(4, out_w, XL // 2, XL)
+    for copy in extras:
+        copy.wait()
+    whole = extra_in[0]
+    for s in range(1, D):
+        whole = whole + extra_in[s]
     column = jnp.zeros((XL, 1), f32)
     for r in range(N // 128):
         spot = lax.broadcasted_iota(jnp.int32, (XL, 128), 1) + r * 128
@@ -361,34 +372,39 @@
     for x in range(XL):
         i, rows = line(x)
         state = spec[i, rows, :] + q * state
-        snd_i = pl.ds(0, KB)
-        back[x, snd_i, :] = state
+        back[x] = state
     state = cplane[1]
     for x in range(XL - 1, -1, -1):
         i, rows = line(x)
         value = spec[i, rows, :]
         ahead = q * state
         state = value + ahead
-        spec[i, rows, :] = factor * (back[x, 0:KB, :] + ahead)
+        spec[i, rows, :] = factor * (back[x] + ahead)
         spec[i, rows.start : rows.start + 1, 0:128] += column[x : x + 1, :]
 
     slabs = got
 
-    def unfourier(i, _):
+    copies = []
+    for i in range(XP):
         high, low = two(spec[i])
         slabs[i] = dot_nt(four_h[...], high) + dot_nt(four_h[...], low) + dot_nt(four_l[...], high)
-        return 0
-
-    lax.fori_loop(0, XP, unfourier, 0)
-    copies = []
-    for n, peer in enumerate(gy_peers):
-        part = pl.ds(pl.multiple_of(peer * YL, YL), YL)
-        copies.append(
-            remote(slabs.at[:, part, :], back_in.at[iy], ret_send.at[n], ret_recv.at[n], (ix, peer))
-        )
-    back_in[iy] = slabs[:, mine, :]
+        for n, peer in enumerate(gy_peers):
+            part = pl.ds(pl.multiple_of(peer * YL, YL), YL)
+            slot = i * G + n
+            copies.append(
+                remote(slabs.at[i, part, :], back_in.at[iy, i], ret_send.at[slot], ret_recv.at[slot], (ix, peer))
+            )
+        back_in[iy, i] = slabs[i, mine, :]
     for copy in copies:
         copy.wait()
+
+
+def finish(G, back_in, full_h, full_l, *refs):
+    sources, (out_p, *targets), sems = refs[:5], refs[5:11], refs[11]
+    copies = [pltpu.make_async_copy(a, b, sems.at[n]) for n, (a, b) in enumerate(zip(sources, targets))]
+    for copy in copies:
+        copy.start()
+    _, XP, YL, Z = back_in.shape
     rhs = [two(back_in[g].reshape(XP * YL, Z)) for g in range(G)]
     for h in range(G):
         rows = slice(h * Z, (h + 1) * Z)
@@ -398,6 +414,8 @@
             high, low = rhs[g]
             part = part + dot_nt(high, full_h[rows, cols]) + dot_nt(high, full_l[rows, cols]) + dot_nt(low, full_h[rows, cols])
         out_p[h * XP : (h + 1) * XP] = part.reshape(XP, YL, Z)
+    for copy in copies:
+        copy.wait()
 
 
 def body(D, G, velocity_x, velocity_y, velocity_z, potential_temp, total_water):
@@ -409,7 +427,7 @@
     V = pltpu.VMEM
     scratch = [
         V((5, XL + 8, YL + 16, Z), f32),
-        V((XL + 8, YL + 16, 3 * Z), f32),
+        V((5, XL + 8, YL + 16, 3 * Z), f32),
         V((2, 5, 4 * XL, Z), f32),
         V((2, 5, 4 * XL, Z), bf16),
         V((2, 5, 4, YL, Z), bf16),
@@ -421,24 +439,27 @@
         V((G, XP, YL, Z), f32),
         V((XP, Y, Z), f32),
         V((XP, Z, Y), f32),
-        V((D, 16, 128), f32),
-        V((D, 16, 128), f32),
+        V((D, ch, 128), f32),
+        V((D, ch, 128), f32),
+        V((8, 128), f32),
+        V((D, 8, 128), f32),
         V((D, ch, 128), f32),
         V((D, ch, 128), f32),
         V((2, KB, Y), f32),
         V((XL, KB, Y), f32),
-        V((G, XP, YL, Z), f32),
         dma((16,)), dma((16,)),
-        dma((G,)), dma((G,)),
+        dma((2 * G,)), dma((2 * G,)),
         dma((D,)), dma((D,)),
         dma((D,)), dma((D,)),
-        dma((G,)), dma((G,)),
+        dma((D,)), dma((D,)),
+        dma((XP * G,)), dma((XP * G,)),
     ]
     block = jax.ShapeDtypeStruct((XL, YL, Z), bf16)
     vmem = pl.BlockSpec(memory_space=pltpu.VMEM)
-    return pl.pallas_call(
+    where = pl.BlockSpec(memory_space=pl.ANY)
+    *stars, modes = pl.pallas_call(
         functools.partial(kernel, D, G, XL, YL, Z),
-        out_shape=(block,) * 5 + (jax.ShapeDtypeStruct((XL, YL, Z), f32),),
+        out_shape=(block,) * 5 + (jax.ShapeDtypeStruct((G, XP, YL, Z), f32),),
         in_specs=[vmem] * (5 + len(tables)),
         out_specs=(vmem,) * 6,
         scratch_shapes=scratch,
@@ -446,6 +467,15 @@
             collective_id=0, has_side_effects=True, vmem_limit_bytes=56 * 1024 * 1024
         ),
     )(velocity_x, velocity_y, velocity_z, potential_temp, total_water, *tables)
+    pressure, *stars = pl.pallas_call(
+        functools.partial(finish, G),
+        out_shape=(jax.ShapeDtypeStruct((XL, YL, Z), f32),) + (block,) * 5,
+        in_specs=[vmem] * 3 + [where] * 5,
+        out_specs=(vmem,) + (where,) * 5,
+        scratch_shapes=[dma((5,))],
+        compiler_params=pltpu.CompilerParams(vmem_limit_bytes=40 * 1024 * 1024),
+    )(modes, tables[1], tables[2], *stars)
+    return (*stars, pressure)
 
 
 def solution(mesh):

time: 61 us -> 57.7 us (0.946)
  Pallas kernels: 54.1 us -> 50.9 us
    pallas_call x1, Pallas kernels: 54.1 us -> 48.9 us  [body(): pl.pallas_call(functools.partial(kernel, D, G, XL, YL, Z), out_shape=(blo...]
    pallas_call x0 -> x1, Pallas kernels: none -> 1.98 us  [body(): pl.pallas_call(functools.partial(finish, G), out_shape=(jax.ShapeDtypeStr...]
where the time goes in v2:
time: 57.7 us; the launch traced here: 57.3 us
  Pallas kernels  50.9 us (88%)
  local copies, waits for them, and re-layouts  5.8 us (10%)
  between operations  0.69 us (1%)
    pallas_call x1, Pallas kernels, body(): pl.pallas_call(functools.partial(kernel, D, G, XL, YL, Z), out_shape=(blo...  48.9 us
    unnamed x16, local copies, waits for them, and re-layouts  5.8 us
    pallas_call x1, Pallas kernels, body(): pl.pallas_call(functools.partial(finish, G), out_shape=(jax.ShapeDtypeStr...  1.98 us

profile of v2, /device:TPU:0, one launch (start us, length us, event | category | flops | bytes accessed | tf_op | source)
XLA Modules:
  0.0 57.3 jit_solution(6326592525483396029)
XLA Ops:
  0.6 0.0 copy-start
  0.6 0.0 copy-start.1
  0.7 48.9 %shard_map.190 = (bf16[16,64,128]{2,1,0:T(8,128)(2,1)}, bf16[16,64,128]{2,1,0:T(8,128)(2,1)}, bf16[16,64,128]{2,1,0:T(8,128)(2,1)}, bf16[16,64,128]{2,1,0:T(8,12...) custom-call(bf16[16,64,128]{2,1,0:T(8,128)(2,1)} %refs_0_.1, bf16[16,64,128]{2,1,0:T(8,128)(2,1)} %refs_1_.1, ...), custom_call_target="tpu_custom_call" | custom-call | tf_op jit(solution)/shard_map/pallas_call | solution.py:460
  49.5 0.0 copy-done
  49.6 0.0 copy-done.1
  49.6 0.0 copy-start.2
  49.6 1.0 %copy-done.2 = f32[2,8,64,128]{3,2,1,0:T(8,128)S(1)} copy-done((f32[2,8,64,128]{3,2,1,0:T(8,128)S(1)}, f32[2,8,64,128]{3,2,1,0:T(8,128)}, u32[]{:S(2)}) %copy-start.2) | copy-done | bytes 524312
  50.6 0.0 copy-start.3
  50.6 0.9 %copy-done.3 = bf16[16,64,128]{2,1,0:T(8,128)(2,1)S(1)} copy-done((bf16[16,64,128]{2,1,0:T(8,128)(2,1)S(1)}, bf16[16,64,128]{2,1,0:T(8,128)(2,1)}, u32[]{:S(2)}) %copy-start.3) | copy-done | bytes 262168
  51.6 0.0 copy-start.4
  51.6 0.9 %copy-done.4 = bf16[16,64,128]{2,1,0:T(8,128)(2,1)S(1)} copy-done((bf16[16,64,128]{2,1,0:T(8,128)(2,1)S(1)}, bf16[16,64,128]{2,1,0:T(8,128)(2,1)}, u32[]{:S(2)}) %copy-start.4) | copy-done | bytes 262168
  52.5 0.0 copy-start.5
  52.5 0.9 %copy-done.5 = bf16[16,64,128]{2,1,0:T(8,128)(2,1)S(1)} copy-done((bf16[16,64,128]{2,1,0:T(8,128)(2,1)S(1)}, bf16[16,64,128]{2,1,0:T(8,128)(2,1)}, u32[]{:S(2)}) %copy-start.5) | copy-done | bytes 262168
  53.5 0.0 copy-start.6
  53.5 0.9 %copy-done.6 = bf16[16,64,128]{2,1,0:T(8,128)(2,1)S(1)} copy-done((bf16[16,64,128]{2,1,0:T(8,128)(2,1)S(1)}, bf16[16,64,128]{2,1,0:T(8,128)(2,1)}, u32[]{:S(2)}) %copy-start.6) | copy-done | bytes 262168
  54.4 0.0 copy-start.7
  54.4 0.9 %copy-done.7 = bf16[16,64,128]{2,1,0:T(8,128)(2,1)S(1)} copy-done((bf16[16,64,128]{2,1,0:T(8,128)(2,1)S(1)}, bf16[16,64,128]{2,1,0:T(8,128)(2,1)}, u32[]{:S(2)}) %copy-start.7) | copy-done | bytes 262168
  55.4 2.0 %shard_map.191 = (f32[16,64,128]{2,1,0:T(8,128)}, bf16[16,64,128]{2,1,0:T(8,128)(2,1)}, bf16[16,64,128]{2,1,0:T(8,128)(2,1)}, bf16[16,64,128]{2,1,0:T(8,128)(2,1...) custom-call(f32[2,8,64,128]{3,2,1,0:T(8,128)S(1)} %copy-done.2, bf16[256,256]{1,0:T(8,128)(2,1)S(1)} %copy-done.1, ...), custom_call_target="tpu_custom_call" | custom-call | tf_op jit(solution)/shard_map/pallas_call | solution.py:470
Async XLA Ops:
  0.6 48.9 %copy-start = (bf16[256,256]{1,0:T(8,128)(2,1)S(1)}, bf16[256,256]{1,0:T(8,128)(2,1)}, u32[]{:S(2)}) copy-start(bf16[256,256]{1,0:T(8,128)(2,1)} %constant.22.clone.refs_7_.full_l) | copy-start | bytes 393220
  0.6 48.9 %copy-start.1 = (bf16[256,256]{1,0:T(8,128)(2,1)S(1)}, bf16[256,256]{1,0:T(8,128)(2,1)}, u32[]{:S(2)}) copy-start(bf16[256,256]{1,0:T(8,128)(2,1)} %constant.21.clone.refs_6_.full_h) | copy-start | bytes 393220
  49.6 1.0 %copy-start.2 = (f32[2,8,64,128]{3,2,1,0:T(8,128)S(1)}, f32[2,8,64,128]{3,2,1,0:T(8,128)}, u32[]{:S(2)}) copy-start(f32[2,8,64,128]{3,2,1,0:T(8,128)} %get-tuple-element.18.back_in) | copy-start | bytes 1572868
  50.6 0.9 %copy-start.3 = (bf16[16,64,128]{2,1,0:T(8,128)(2,1)S(1)}, bf16[16,64,128]{2,1,0:T(8,128)(2,1)}, u32[]{:S(2)}) copy-start(bf16[16,64,128]{2,1,0:T(8,128)(2,1)} %get-tuple-element.19.refs_0_) | copy-start | bytes 786436
  51.6 0.9 %copy-start.4 = (bf16[16,64,128]{2,1,0:T(8,128)(2,1)S(1)}, bf16[16,64,128]{2,1,0:T(8,128)(2,1)}, u32[]{:S(2)}) copy-start(bf16[16,64,128]{2,1,0:T(8,128)(2,1)} %get-tuple-element.20.refs_1_) | copy-start | bytes 786436
  52.5 0.9 %copy-start.5 = (bf16[16,64,128]{2,1,0:T(8,128)(2,1)S(1)}, bf16[16,64,128]{2,1,0:T(8,128)(2,1)}, u32[]{:S(2)}) copy-start(bf16[16,64,128]{2,1,0:T(8,128)(2,1)} %get-tuple-element.21.refs_2_) | copy-start | bytes 786436
  53.5 0.9 %copy-start.6 = (bf16[16,64,128]{2,1,0:T(8,128)(2,1)S(1)}, bf16[16,64,128]{2,1,0:T(8,128)(2,1)}, u32[]{:S(2)}) copy-start(bf16[16,64,128]{2,1,0:T(8,128)(2,1)} %get-tuple-element.22.refs_3_) | copy-start | bytes 786436
  54.4 0.9 %copy-start.7 = (bf16[16,64,128]{2,1,0:T(8,128)(2,1)S(1)}, bf16[16,64,128]{2,1,0:T(8,128)(2,1)}, u32[]{:S(2)}) copy-start(bf16[16,64,128]{2,1,0:T(8,128)(2,1)} %get-tuple-element.23.refs_4_) | copy-start | bytes 786436

commit v3 on v2

--- a/solution.py
+++ b/solution.py
@@ -154,15 +154,21 @@
         halos.append(remote(src_ref, dst_ref, halo_send.at[slot], halo_recv.at[slot], device))
 
     lines = 4 * XL
-    for f in range(5):
+    halo(ysend.at[1, 0:3], yhalo.at[0, 0:3], (ix, above))
+    halo(ysend.at[0, 0:3], yhalo.at[1, 0:3], (ix, below))
+    halo(ysend.at[1, 0:3, lines - 16 : lines], corner.at[0], (right, above))
+    halo(ysend.at[0, 0:3, lines - 16 : lines], corner.at[1], (right, below))
+    halo(ysend.at[1, 0:3, 0:16], corner.at[2], (left, above))
+    halo(ysend.at[0, 0:3, 0:16], corner.at[3], (left, below))
+    for f in range(3):
         halo(fields[f].at[XL - 4 : XL], xhalo.at[0, f], (right, iy))
         halo(fields[f].at[0:4], xhalo.at[1, f], (left, iy))
-    halo(ysend.at[1], yhalo.at[0], (ix, above))
-    halo(ysend.at[0], yhalo.at[1], (ix, below))
-    halo(ysend.at[1, :, lines - 16 : lines], corner.at[0], (right, above))
-    halo(ysend.at[0, :, lines - 16 : lines], corner.at[1], (right, below))
-    halo(ysend.at[1, :, 0:16], corner.at[2], (left, above))
-    halo(ysend.at[0, :, 0:16], corner.at[3], (left, below))
+    wind_halos = len(halos)
+    halo(ysend.at[1, 3:5], yhalo.at[0, 3:5], (ix, above))
+    halo(ysend.at[0, 3:5], yhalo.at[1, 3:5], (ix, below))
+    for f in range(3, 5):
+        halo(fields[f].at[XL - 4 : XL], xhalo.at[0, f], (right, iy))
+        halo(fields[f].at[0:4], xhalo.at[1, f], (left, iy))
 
     for f in range(5):
         pad[f, :, 0:8, :] = jnp.zeros((XL + 8, 8, Z), f32)
@@ -175,20 +181,23 @@
             return 0
 
         lax.fori_loop(0, XL // 4, along_z, 0)
-    for copy in halos:
-        copy.wait()
-    for f in range(5):
+    def unpack(f):
         pad[f, 0:4, 8 : YL + 8, :] = xhalo[0, f].astype(f32)
         pad[f, XL + 4 : XL + 8, 8 : YL + 8, :] = xhalo[1, f].astype(f32)
         for side, row in ((0, 4), (1, YL + 8)):
             strip = yhalo[side, f].astype(f32)
             for x in range(XL):
                 pad[f, 4 + x, row : row + 4, :] = strip[4 * x : 4 * x + 4]
-            for far, start in ((0, 0), (2, XL + 4)):
-                strip_c = corner[far + side, f].astype(f32)
-                for x in range(4):
-                    pad[f, start + x, row : row + 4, :] = strip_c[4 * x : 4 * x + 4]
-
+            if f < 3:
+                for far, start in ((0, 0), (2, XL + 4)):
+                    strip_c = corner[far + side, f].astype(f32)
+                    for x in range(4):
+                        pad[f, start + x, row : row + 4, :] = strip_c[4 * x : 4 * x + 4]
+
+    for copy in halos[:wind_halos]:
+        copy.wait()
+    for f in range(3):
+        unpack(f)
     outer = jnp.concatenate([pad[0, 3, 8 : YL + 8, :], pad[0, XL + 4, 8 : YL + 8, :]], axis=0)
     outer = dot(outer.astype(bf16), band[...])
     zbuf[0, 3, 8 : YL + 8, :] = outer[0:YL]
@@ -221,42 +230,50 @@
             result = result + time_step * pad[3, px, here, :]
         return result
 
-    def step_x(x, _):
-        for start in range(0, YL, 16):
-            sx[x, start : start + 16, :] = star(0, x + 3, start, 16)
-        return 0
-
-    lax.fori_loop(0, XL + 2, step_x, 0)
-
-    def step_y(x, _):
-        for start in range(-1, YL - 16, 16):
-            sy[x, start + 8 : start + 24, :] = star(1, x + 4, start, 16)
-        sy[x, YL + 1 : YL + 9, :] = star(1, x + 4, YL - 7, 8)
-        return 0
-
-    lax.fori_loop(0, XL, step_y, 0)
     lane = lax.broadcasted_iota(jnp.int32, (16, Z), 1)
-
-    def step_z(x, _):
-        for start in range(0, YL, 16):
-            here = pl.ds(start, 16)
-            value = star(2, x + 4, start, 16)
-            out_z[x, here, :] = value.astype(bf16)
-            out_x[x, here, :] = sx[x + 1, here, :].astype(bf16)
-            out_y[x, here, :] = sy[x, pl.ds(start + 8, 16), :].astype(bf16)
-            up = jnp.where(lane < Z - 1, pltpu.roll(value, Z - 1, 1), 0.0)
-            down = jnp.where(lane > 0, pltpu.roll(value, 1, 1), 0.0)
-            grad = (sx[x + 2, here, :] - sx[x, here, :]) + (up - down)
-            grad = grad + (sy[x, pl.ds(start + 9, 16), :] - sy[x, pl.ds(start + 7, 16), :])
-            src[x, here, :] = grad * (0.5 / time_step)
-        return 0
-
-    lax.fori_loop(0, XL, step_z, 0)
-
+    parts = min(4, XP)
+    half = XP // parts
     mine = pl.ds(pl.multiple_of(iy * YL, YL), YL)
-    half = XP // 2
+
+    def winds(c):
+        wide = half + 2 if c == 0 else half
+        offset = 0 if c == 0 else c * half + 2
+
+        def step_x(j, _):
+            x = (j // wide) * XP + offset + j % wide
+            for start in range(0, YL, 16):
+                sx[x, start : start + 16, :] = star(0, x + 3, start, 16)
+            return 0
+
+        def step_y(j, _):
+            x = (j // half) * XP + c * half + j % half
+            for start in range(-1, YL - 16, 16):
+                sy[x, start + 8 : start + 24, :] = star(1, x + 4, start, 16)
+            sy[x, YL + 1 : YL + 9, :] = star(1, x + 4, YL - 7, 8)
+            return 0
+
+        def step_z(j, _):
+            x = (j // half) * XP + c * half + j % half
+            for start in range(0, YL, 16):
+                here = pl.ds(start, 16)
+                value = star(2, x + 4, start, 16)
+                out_z[x, here, :] = value.astype(bf16)
+                out_x[x, here, :] = sx[x + 1, here, :].astype(bf16)
+                out_y[x, here, :] = sy[x, pl.ds(start + 8, 16), :].astype(bf16)
+                up = jnp.where(lane < Z - 1, pltpu.roll(value, Z - 1, 1), 0.0)
+                down = jnp.where(lane > 0, pltpu.roll(value, 1, 1), 0.0)
+                grad = (sx[x + 2, here, :] - sx[x, here, :]) + (up - down)
+                grad = grad + (sy[x, pl.ds(start + 9, 16), :] - sy[x, pl.ds(start + 7, 16), :])
+                src[x, here, :] = grad * (0.5 / time_step)
+            return 0
+
+        lax.fori_loop(0, G * wide, step_x, 0)
+        lax.fori_loop(0, G * half, step_y, 0)
+        lax.fori_loop(0, G * half, step_z, 0)
+
     copies = []
-    for c in range(2):
+    for c in range(parts):
+        winds(c)
         planes = slice(c * half, (c + 1) * half)
         lhs = [two(src[h * XP + c * half : h * XP + (c + 1) * half].reshape(half * YL, Z)) for h in range(G)]
         for g in range(G):
@@ -273,6 +290,11 @@
         ])
         got[planes, mine, :] = snd[iy, planes]
 
+    for copy in halos[wind_halos:]:
+        copy.wait()
+    for f in range(3, 5):
+        unpack(f)
+
     def scalar(f, target, first, last):
         def step_s(x, _):
             for start in range(0, YL, 16):
@@ -281,14 +303,14 @@
 
         lax.fori_loop(first, last, step_s, 0)
 
-    scalar(3, out_t, 0, XL)
+    scalar(3, out_t, 0, XL // 2)
 
     def fourier(i, _):
         high, low = two(got[i].T)
         spec[i] = dot(high, four_h[...]) + dot(high, four_l[...]) + dot(low, four_h[...])
         return 0
 
-    for c in range(2):
+    for c in range(parts):
         for copy in copies[c]:
             copy.wait()
         lax.fori_loop(c * half, (c + 1) * half, fourier, 0)
@@ -331,7 +353,8 @@
         extras.append(remote(extra_out, extra_in.at[ix], ext_send.at[n], ext_recv.at[n], (peer, iy)))
     extra_in[ix] = extra
     ends_in[slot_of(ix, ix)] = ends[ix]
-    scalar(4, out_w, 0, XL // 2)
+    scalar(3, out_t, XL // 2, XL)
+    scalar(4, out_w, 0, XL // 4)
     for copy in copies:
         copy.wait()
     jump_t, wrap_t = jump[iy, ix], wrap[iy, ix]
@@ -349,7 +372,7 @@
             remote(carry.at[slot_of(peer, ix)], carry_in.at[ix], car_send.at[n], car_recv.at[n], (peer, iy))
         )
     carry_in[ix] = carry[slot_of(ix, ix)]
-    scalar(4, out_w, XL // 2, XL)
+    scalar(4, out_w, XL // 4, XL)
     for copy in extras:
         copy.wait()
     whole = extra_in[0]
@@ -400,10 +423,14 @@
 
 
 def finish(G, back_in, full_h, full_l, *refs):
-    sources, (out_p, *targets), sems = refs[:5], refs[5:11], refs[11]
-    copies = [pltpu.make_async_copy(a, b, sems.at[n]) for n, (a, b) in enumerate(zip(sources, targets))]
-    for copy in copies:
+    sources, (out_p, *targets), held, came, left = refs[:5], refs[5:11], refs[11], refs[12], refs[13]
+    fetched = [pltpu.make_async_copy(a, held.at[n], came.at[n]) for n, a in enumerate(sources)]
+    copies = [pltpu.make_async_copy(held.at[n], b, left.at[n]) for n, b in enumerate(targets)]
+    for copy in fetched:
         copy.start()
+    for first, second in zip(fetched, copies):
+        first.wait()
+        second.start()
     _, XP, YL, Z = back_in.shape
     rhs = [two(back_in[g].reshape(XP * YL, Z)) for g in range(G)]
     for h in range(G):
@@ -432,7 +459,7 @@
         V((2, 5, 4 * XL, Z), bf16),
         V((2, 5, 4, YL, Z), bf16),
         V((2, 5, 4 * XL, Z), bf16),
-        V((4, 5, 16, Z), bf16),
+        V((4, 3, 16, Z), bf16),
         V((XL + 2, YL, Z), f32),
         V((XL, YL + 16, Z), f32),
         V((XL, YL, Z), f32),
@@ -447,8 +474,8 @@
         V((D, ch, 128), f32),
         V((2, KB, Y), f32),
         V((XL, KB, Y), f32),
-        dma((16,)), dma((16,)),
-        dma((2 * G,)), dma((2 * G,)),
+        dma((18,)), dma((18,)),
+        dma((4 * G,)), dma((4 * G,)),
         dma((D,)), dma((D,)),
         dma((D,)), dma((D,)),
         dma((D,)), dma((D,)),
@@ -456,7 +483,7 @@
     ]
     block = jax.ShapeDtypeStruct((XL, YL, Z), bf16)
     vmem = pl.BlockSpec(memory_space=pltpu.VMEM)
-    where = pl.BlockSpec(memory_space=pl.ANY)
+    where = pl.BlockSpec(memory_space=pltpu.HBM)
     *stars, modes = pl.pallas_call(
         functools.partial(kernel, D, G, XL, YL, Z),
         out_shape=(block,) * 5 + (jax.ShapeDtypeStruct((G, XP, YL, Z), f32),),
@@ -472,8 +499,8 @@
         out_shape=(jax.ShapeDtypeStruct((XL, YL, Z), f32),) + (block,) * 5,
         in_specs=[vmem] * 3 + [where] * 5,
         out_specs=(vmem,) + (where,) * 5,
-        scratch_shapes=[dma((5,))],
-        compiler_params=pltpu.CompilerParams(vmem_limit_bytes=40 * 1024 * 1024),
+        scratch_shapes=[V((5, XL, YL, Z), bf16), dma((5,)), dma((5,))],
+        compiler_params=pltpu.CompilerParams(vmem_limit_bytes=60 * 1024 * 1024),
     )(modes, tables[1], tables[2], *stars)
     return (*stars, pressure)
 

time: 57.7 us -> 49.8 us (0.86)
  local copies, waits for them, and re-layouts: 5.8 us -> 0 us
  Pallas kernels: 50.9 us -> 49 us
    unnamed x16 -> x0, local copies, waits for them, and re-layouts: 5.8 us -> none
    pallas_call x1, Pallas kernels: 48.9 us -> 45 us  [body(): pl.pallas_call(functools.partial(kernel, D, G, XL, YL, Z), out_shape=(blo...]
    pallas_call x1, Pallas kernels: 1.98 us -> 4.01 us  [body(): pl.pallas_call(functools.partial(finish, G), out_shape=(jax.ShapeDtypeStr...]
where the time goes in v3:
time: 49.8 us; the launch traced here: 49.6 us
  Pallas kernels  49 us (98%)
  between operations  0.64 us (1%)
    pallas_call x1, Pallas kernels, body(): pl.pallas_call(functools.partial(kernel, D, G, XL, YL, Z), out_shape=(blo...  45 us
    pallas_call x1, Pallas kernels, body(): pl.pallas_call(functools.partial(finish, G), out_shape=(jax.ShapeDtypeStr...  4.01 us

profile of v3, /device:TPU:0, one launch (start us, length us, event | category | flops | bytes accessed | tf_op | source)
XLA Modules:
  0.0 49.6 jit_solution(699464251406578179)
XLA Ops:
  0.6 45.0 %shard_map.190 = (bf16[16,64,128]{2,1,0:T(8,128)(2,1)}, bf16[16,64,128]{2,1,0:T(8,128)(2,1)}, bf16[16,64,128]{2,1,0:T(8,128)(2,1)}, bf16[16,64,128]{2,1,0:T(8,12...) custom-call(bf16[16,64,128]{2,1,0:T(8,128)(2,1)} %refs_0_.1, bf16[16,64,128]{2,1,0:T(8,128)(2,1)} %refs_1_.1, ...), custom_call_target="tpu_custom_call" | custom-call | tf_op jit(solution)/shard_map/pallas_call | solution.py:487
  45.6 4.0 %shard_map.191 = (f32[16,64,128]{2,1,0:T(8,128)}, bf16[16,64,128]{2,1,0:T(8,128)(2,1)}, bf16[16,64,128]{2,1,0:T(8,128)(2,1)}, bf16[16,64,128]{2,1,0:T(8,128)(2,1...) custom-call(f32[2,8,64,128]{3,2,1,0:T(8,128)} %get-tuple-element.18.back_in, ...), custom_call_target="tpu_custom_call" | custom-call | tf_op jit(solution)/shard_map/pallas_call | solution.py:497
